TPU v7x, 32 devices: a whole 2x2x4 slice. The times are simulated.
32 devices in a mesh: seq: 4 (over z), fsdp: 8 (over y, x, core).
Axes of the slice: x: 2, y: 2, z: 4, core: 2. Of those that a mesh axis runs over, the one named last changes fastest.
Arguments:
- tokens: bfloat16 [4096, 1024], P(('fsdp', 'seq')), may hold values from -6 to 6
- cotangent: bfloat16 [4096, 1024], P(('fsdp', 'seq')), may hold values from -6 to 6
- doc_starts: int32 [8], replicated, may hold values from 0 to 4095, as said below
- variate_ids: int32 [4096], replicated, may hold values from 0 to 7, as said below
- time_ids: int32 [4096], replicated, may hold values from 0 to 63, as said below
- gain_attn: float32 [1024], replicated, may hold values from 0.5 to 1.5
- w_attn: bfloat16 [1024, 3072], P('fsdp'), may hold values from -0.1875 to 0.1875
- gain_query: float32 [64], replicated, may hold values from 0.5 to 1.5
- gain_key: float32 [64], replicated, may hold values from 0.5 to 1.5
- variate_bias: float32 [16, 2], replicated, may hold values from -3 to 3
- w_output: bfloat16 [1024, 1024], P('fsdp'), may hold values from -3 to 3
- gain_feed: float32 [1024], replicated, may hold values from 0.5 to 1.5
- w_gate: bfloat16 [1024, 4096], P('fsdp'), may hold values from -0.1875 to 0.1875
- w_up: bfloat16 [1024, 4096], P('fsdp'), may hold values from -0.1875 to 0.1875
- w_down: bfloat16 [4096, 1024], P('fsdp'), may hold values from -0.09375 to 0.09375
Outputs:
- layer_out: bfloat16 [4096, 1024], P(('fsdp', 'seq'))
- tokens_grad: float32 [4096, 1024], P(('fsdp', 'seq'))
- attn_grad: float32 [1024, 3072], P(('seq', 'fsdp'))
- output_grad: float32 [1024, 1024], P(('seq', 'fsdp'))
- gate_grad: float32 [1024, 4096], P(('seq', 'fsdp'))
- up_grad: float32 [1024, 4096], P(('seq', 'fsdp'))
- down_grad: float32 [4096, 1024], P(('seq', 'fsdp'))
- attn_gain_grad: float32 [1024], P(('seq', 'fsdp'))
- feed_gain_grad: float32 [1024], P(('seq', 'fsdp'))
- query_gain_grad: float32 [64], replicated
- key_gain_grad: float32 [64], replicated
- bias_grad: float32 [16, 2], replicated
Inputs may be any that keep to these rules, and one draw needn't show every extreme that they name: `doc_starts`: non-decreasing, the first entry is 0. `variate_ids`: only compared for equality within a document. `time_ids`: a time index modulo 64; token 0 has 63.
All inputs are finite; a program needn't handle non-finite values.
Results may differ from a plain program's by a relative error of at most 0.038.
Values may be sent and summed in bfloat16 or wider, within the bound.
A program may use at most 256 MiB of HBM per device.

v0:
```python
import jax
import jax.numpy as jnp
from jax import lax
from jax.sharding import PartitionSpec as P

EPSILON = 1e-06
NEG_FILL = -1e30


def rms_scale(vector, gain):
    return vector * lax.rsqrt(jnp.mean(vector * vector, axis=-1, keepdims=True) + EPSILON) * gain


def rotate(vector, angles):
    half_width = vector.shape[-1] // 2
    front_half = vector[..., :half_width]
    back_half = vector[..., half_width:]
    cosine = jnp.cos(angles)
    sine_part = jnp.sin(angles)
    return jnp.concatenate(
        [front_half * cosine - back_half * sine_part, front_half * sine_part + back_half * cosine],
        axis=-1,
    )


def angle_table(times, width):
    half_width = width // 2
    frequency = 10000.0 ** (-2.0 * jnp.arange(half_width, dtype=jnp.float32) / width)
    return times.astype(jnp.float32)[:, None, None] * frequency


def doc_index(positions, starts):
    return jnp.sum((starts[None, :] <= positions[:, None]).astype(jnp.int32), axis=1) - 1


def swiglu(gate_act, up_act):
    return jax.nn.silu(gate_act) * up_act


def per_device(
    tokens,
    cotangent,
    doc_starts,
    variate_ids,
    time_ids,
    gain_attn,
    w_attn,
    gain_query,
    gain_key,
    variate_bias,
    w_output,
    gain_feed,
    w_gate,
    w_up,
    w_down,
):
    seq_count = lax.axis_size("seq")
    fsdp_count = lax.axis_size("fsdp")
    seq_pos = lax.axis_index("seq")
    fsdp_pos = lax.axis_index("fsdp")
    tok_rows = tokens.shape[0]
    head_count = variate_bias.shape[0]
    head_dim = gain_query.shape[0]
    local_heads = head_count // seq_count
    head_lanes = local_heads * head_dim
    group_rows = tok_rows * seq_count
    total_rows = group_rows * fsdp_count
    score_scale = head_dim ** (-0.5)
    full_attn, full_output, full_gate, full_up, full_down = (
        lax.all_gather(w_attn, "fsdp", axis=0, tiled=True),
        lax.all_gather(w_output, "fsdp", axis=0, tiled=True),
        lax.all_gather(w_gate, "fsdp", axis=0, tiled=True),
        lax.all_gather(w_up, "fsdp", axis=0, tiled=True),
        lax.all_gather(w_down, "fsdp", axis=0, tiled=True),
    )
    inputs = tokens.astype(jnp.float32)
    normed_wide, norm_pull = jax.vjp(rms_scale, inputs, gain_attn)
    normed = normed_wide.astype(jnp.bfloat16)
    first_row = (fsdp_pos * seq_count + seq_pos) * tok_rows
    my_times = lax.dynamic_slice_in_dim(time_ids, first_row, tok_rows)
    angles = angle_table(my_times, head_dim)
    projected = jnp.dot(normed, full_attn, preferred_element_type=jnp.float32).reshape(
        tok_rows, 3, head_count, head_dim
    )

    def prepare_local(proj_in, gain_q, gain_k):
        queries = rotate(rms_scale(proj_in[:, 0], gain_q), angles)
        key_rows = rotate(rms_scale(proj_in[:, 1], gain_k), angles)
        return (queries, key_rows)

    (queries, key_rows), prep_pull = jax.vjp(prepare_local, projected, gain_query, gain_key)
    packed = jnp.stack(
        [
            queries.astype(jnp.bfloat16),
            key_rows.astype(jnp.bfloat16),
            projected[:, 2].astype(jnp.bfloat16),
        ],
        axis=1,
    )
    packed = packed.reshape(tok_rows, 3, seq_count, head_lanes)
    grouped = lax.all_to_all(packed, "seq", split_axis=2, concat_axis=0, tiled=True).reshape(
        group_rows, 3, local_heads, head_dim
    )
    q_heads = grouped[:, 0]
    kv_local = grouped[:, 1:].reshape(group_rows, 2, head_lanes)
    group_start = fsdp_pos * group_rows
    q_positions = group_start + jnp.arange(group_rows, dtype=jnp.int32)
    q_docs = doc_index(q_positions, doc_starts)
    q_vars = lax.dynamic_slice_in_dim(variate_ids, group_start, group_rows)
    my_bias = lax.dynamic_slice_in_dim(variate_bias, seq_pos * local_heads, local_heads, 0)

    def pair_scores(query_block, query_docs, query_vars, key_block, key_docs, key_vars):
        products = (
            jnp.einsum("qhd,khd->qhk", query_block, key_block, preferred_element_type=jnp.float32)
            * score_scale
        )
        same_var = query_vars[:, None] == key_vars[None, :]
        allowed = query_docs[:, None] == key_docs[None, :]
        biased = products + jnp.where(
            same_var[:, None, :], my_bias[None, :, 0, None], my_bias[None, :, 1, None]
        )
        return (jnp.where(allowed[:, None, :], biased, NEG_FILL), same_var, allowed)

    def block_scores(key_block, start_row):
        key_count = key_block.shape[0]
        k_positions = start_row + jnp.arange(key_count, dtype=jnp.int32)
        k_docs = doc_index(k_positions, doc_starts)
        k_vars = lax.dynamic_slice_in_dim(variate_ids, start_row, key_count)
        return pair_scores(q_heads, q_docs, q_vars, key_block, k_docs, k_vars)

    def fold_block(running, kv_block, start_row):
        row_top, row_sum, accumulated = running
        key_block = kv_block[:, 0].reshape(-1, local_heads, head_dim)
        value_block = kv_block[:, 1].reshape(-1, local_heads, head_dim)
        scores, same_var, allowed = block_scores(key_block, start_row)
        new_top = jnp.maximum(row_top, jnp.max(scores, axis=-1))
        factor = jnp.exp(row_top - new_top)
        weights = jnp.where(allowed[:, None, :], jnp.exp(scores - new_top[..., None]), 0.0)
        row_sum = row_sum * factor + jnp.sum(weights, axis=-1)
        accumulated = accumulated * factor[..., None] + jnp.einsum(
            "qhk,khd->qhd",
            weights.astype(jnp.bfloat16),
            value_block,
            preferred_element_type=jnp.float32,
        )
        return (new_top, row_sum, accumulated)

    start_carry = (
        jnp.full((group_rows, local_heads), NEG_FILL, jnp.float32),
        jnp.zeros((group_rows, local_heads), jnp.float32),
        jnp.zeros((group_rows, local_heads, head_dim), jnp.float32),
    )
    key_piece = lax.all_gather(kv_local, "fsdp", axis=0, tiled=True)
    piece_count = key_piece.shape[0] // group_rows

    def one_step(block_index, inner_carry):
        piece_part = lax.dynamic_slice_in_dim(key_piece, block_index * group_rows, group_rows, 0)
        return fold_block(inner_carry, piece_part, block_index * group_rows)

    folded = lax.fori_loop(0, piece_count, one_step, start_carry)
    row_top, row_sum, accumulated = folded
    log_sum = row_top + jnp.log(row_sum)
    attended = accumulated / row_sum[..., None]
    heads_low = attended.reshape(group_rows, 1, head_lanes).astype(jnp.bfloat16)
    heads_out = lax.all_to_all(heads_low, "seq", split_axis=0, concat_axis=1, tiled=True).reshape(
        tok_rows, head_count * head_dim
    )
    middle = inputs + jnp.dot(heads_out, full_output, preferred_element_type=jnp.float32)
    normed_mid_wide, mid_pull = jax.vjp(rms_scale, middle, gain_feed)
    normed_mid = normed_mid_wide.astype(jnp.bfloat16)
    gate_act = jnp.dot(normed_mid, full_gate, preferred_element_type=jnp.float32)
    up_act = jnp.dot(normed_mid, full_up, preferred_element_type=jnp.float32)
    hidden_wide, swiglu_pull = jax.vjp(swiglu, gate_act, up_act)
    hidden = hidden_wide.astype(jnp.bfloat16)
    layer_out = (middle + jnp.dot(hidden, full_down, preferred_element_type=jnp.float32)).astype(
        jnp.bfloat16
    )
    down_grad = jnp.dot(hidden.T, cotangent, preferred_element_type=jnp.float32)
    hidden_grad = jnp.dot(cotangent, full_down.T, preferred_element_type=jnp.float32)
    gate_back, up_back = swiglu_pull(hidden_grad)
    gate_low = gate_back.astype(jnp.bfloat16)
    up_low = up_back.astype(jnp.bfloat16)
    gate_grad = jnp.dot(normed_mid.T, gate_low, preferred_element_type=jnp.float32)
    up_grad = jnp.dot(normed_mid.T, up_low, preferred_element_type=jnp.float32)
    normed_mid_grad = jnp.dot(gate_low, full_gate.T, preferred_element_type=jnp.float32) + jnp.dot(
        up_low, full_up.T, preferred_element_type=jnp.float32
    )
    middle_part, feed_gain_grad = mid_pull(normed_mid_grad)
    middle_grad = cotangent.astype(jnp.float32) + middle_part
    middle_low = middle_grad.astype(jnp.bfloat16)
    output_grad = jnp.dot(heads_out.T, middle_low, preferred_element_type=jnp.float32)
    heads_grad = (
        jnp.dot(middle_low, full_output.T, preferred_element_type=jnp.float32)
        .astype(jnp.bfloat16)
        .reshape(tok_rows, seq_count, head_lanes)
    )
    grad_heads = lax.all_to_all(heads_grad, "seq", split_axis=1, concat_axis=0, tiled=True).reshape(
        group_rows, local_heads, head_dim
    )
    row_delta = jnp.sum(grad_heads.astype(jnp.float32) * attended, axis=-1)
    kv_all = lax.all_gather(kv_local, "fsdp", axis=0, tiled=True)

    def back_block(running, block_index):
        query_acc, bias_acc = running
        start_row = block_index * group_rows
        piece_part = lax.dynamic_slice_in_dim(kv_all, start_row, group_rows, 0)
        key_block = piece_part[:, 0].reshape(group_rows, local_heads, head_dim)
        value_block = piece_part[:, 1].reshape(group_rows, local_heads, head_dim)
        scores, same_var, allowed = block_scores(key_block, start_row)
        soft_probs = jnp.where(allowed[:, None, :], jnp.exp(scores - log_sum[..., None]), 0.0)
        prob_grad = jnp.einsum(
            "qhd,khd->qhk", grad_heads, value_block, preferred_element_type=jnp.float32
        )
        score_grad = (soft_probs * (prob_grad - row_delta[..., None])).astype(jnp.bfloat16)
        query_acc = (
            query_acc
            + jnp.einsum("qhk,khd->qhd", score_grad, key_block, preferred_element_type=jnp.float32)
            * score_scale
        )
        wide_grad = score_grad.astype(jnp.float32)
        same_sum = jnp.sum(jnp.where(same_var[:, None, :], wide_grad, 0.0), axis=(0, 2))
        every_sum = jnp.sum(wide_grad, axis=(0, 2))
        bias_acc = bias_acc + jnp.stack([same_sum, every_sum - same_sum], axis=1)
        value_grad = jnp.einsum(
            "qhk,qhd->khd",
            soft_probs.astype(jnp.bfloat16),
            grad_heads,
            preferred_element_type=jnp.float32,
        )
        key_grad = (
            jnp.einsum("qhk,qhd->khd", score_grad, q_heads, preferred_element_type=jnp.float32)
            * score_scale
        )
        block_grads = jnp.stack([key_grad, value_grad], axis=1).reshape(group_rows, 2, head_lanes)
        return ((query_acc, bias_acc), block_grads)

    back_start = (
        jnp.zeros((group_rows, local_heads, head_dim), jnp.float32),
        jnp.zeros((local_heads, 2), jnp.float32),
    )
    (query_acc, bias_acc), kv_grads = lax.scan(
        back_block, back_start, jnp.arange(fsdp_count, dtype=jnp.int32)
    )
    kv_grads = kv_grads.reshape(total_rows, 2, head_lanes)
    kv_owned = lax.psum_scatter(
        kv_grads.astype(jnp.bfloat16), "fsdp", scatter_dimension=0, tiled=True
    ).astype(jnp.float32)
    head_grads = jnp.concatenate(
        [query_acc.reshape(group_rows, 1, head_lanes), kv_owned], axis=1
    ).astype(jnp.bfloat16)
    head_grads = head_grads.reshape(group_rows, 3, 1, head_lanes)
    token_grads = (
        lax.all_to_all(head_grads, "seq", split_axis=0, concat_axis=2, tiled=True)
        .reshape(tok_rows, 3, head_count, head_dim)
        .astype(jnp.float32)
    )
    proj_qk, query_gain_grad, key_gain_grad = prep_pull((token_grads[:, 0], token_grads[:, 1]))
    projected_grad = (
        jnp.concatenate([proj_qk[:, :2], token_grads[:, 2:]], axis=1)
        .reshape(tok_rows, 3 * head_count * head_dim)
        .astype(jnp.bfloat16)
    )
    attn_grad = jnp.dot(normed.T, projected_grad, preferred_element_type=jnp.float32)
    normed_grad = jnp.dot(projected_grad, full_attn.T, preferred_element_type=jnp.float32)
    input_part, attn_gain_grad = norm_pull(normed_grad)
    tokens_grad = middle_grad + input_part
    owned_grads = (
        lax.psum_scatter(attn_grad, ("seq", "fsdp"), scatter_dimension=0, tiled=True),
        lax.psum_scatter(output_grad, ("seq", "fsdp"), scatter_dimension=0, tiled=True),
        lax.psum_scatter(gate_grad, ("seq", "fsdp"), scatter_dimension=0, tiled=True),
        lax.psum_scatter(up_grad, ("seq", "fsdp"), scatter_dimension=0, tiled=True),
        lax.psum_scatter(down_grad, ("seq", "fsdp"), scatter_dimension=0, tiled=True),
        lax.psum_scatter(attn_gain_grad, ("seq", "fsdp"), scatter_dimension=0, tiled=True),
        lax.psum_scatter(feed_gain_grad, ("seq", "fsdp"), scatter_dimension=0, tiled=True),
    )
    bias_full = lax.dynamic_update_slice_in_dim(
        jnp.zeros((head_count, 2), jnp.float32), bias_acc, seq_pos * local_heads, 0
    )
    query_gain_sum, key_gain_sum, bias_grad = lax.psum(
        (query_gain_grad, key_gain_grad, bias_full), ("seq", "fsdp")
    )
    return (
        layer_out,
        tokens_grad,
        owned_grads[0],
        owned_grads[1],
        owned_grads[2],
        owned_grads[3],
        owned_grads[4],
        owned_grads[5],
        owned_grads[6],
        query_gain_sum,
        key_gain_sum,
        bias_grad,
    )


def solution(mesh):
    in_specs = (
        P(("fsdp", "seq"), None),
        P(("fsdp", "seq"), None),
        P(),
        P(),
        P(),
        P(),
        P("fsdp", None),
        P(),
        P(),
        P(),
        P("fsdp", None),
        P(),
        P("fsdp", None),
        P("fsdp", None),
        P("fsdp", None),
    )
    out_specs = (
        P(("fsdp", "seq"), None),
        P(("fsdp", "seq"), None),
        P(("seq", "fsdp"), None),
        P(("seq", "fsdp"), None),
        P(("seq", "fsdp"), None),
        P(("seq", "fsdp"), None),
        P(("seq", "fsdp"), None),
        P(("seq", "fsdp")),
        P(("seq", "fsdp")),
        P(),
        P(),
        P(),
    )
    return jax.shard_map(
        per_device, mesh=mesh, in_specs=in_specs, out_specs=out_specs, check_vma=False
    )
```

profile of v0, /device:TPU:0, one launch (start us, length us, event | category | flops | bytes accessed | tf_op | source)
XLA Modules:
  0.0 1408.2 jit_solution(18161745728923827966)
XLA Ops:
  10.6 47.6 %all-gather.7.cloned.1.call-done = bf16[1024,3072]{1,0:T(8,128)(2,1)} async-done(((bf16[128,3072]{1,0:T(8,128)(2,1)}), bf16[1024,3072]{1,0:T(8,128)(2,1)}) %all-gather.7.cloned.1.call-update) | async-done | bytes 6291472 | tf_op jit(solution)/shard_map/all_gather | solution.py:70
  58.2 5.5 fusion.57
  64.8 24.9 %all_to_all.54 = bf16[128,3,4,256]{0,3,1,2:T(8,128)(2,1)S(1)} all-to-all(bf16[128,3,4,256]{0,3,1,2:T(8,128)(2,1)S(1)} %copy.91), channel_id=1, replica_groups=mesh['seq'=4,'fsdp'=8] {'seq'}, dimensions={2} | all-to-all | bytes 1572864 | tf_op jit(solution)/shard_map/all_to_all | solution.py:101
  95.0 32.2 %all-gather.9.cloned.1.call-done = bf16[4096,2,256]{0,2,1:T(8,128)(2,1)} async-done(((bf16[512,2,256]{0,2,1:T(8,128)(2,1)}), bf16[4096,2,256]{0,2,1:T(8,128)(2,1)}) %all-gather.9.cloned.1.call-update) | async-done | bytes 4194320 | tf_op jit(solution)/shard_map/all_gather | solution.py:153
  127.3 92.7 %while.37 = (s32[]{:T(128)}, f32[512,4]{0,1:T(4,128)S(1)}, f32[512,4]{0,1:T(4,128)S(1)}, f32[512,4,64]{0,2,1:T(8,128)S(1)}, s32[512]{0:T(512)S(1)}, /*index=5*/s...) while((s32[]{:T(128)}, f32[512,4]{0,1:T(4,128)S(1)}, ...), condition=%wide.region_8.9_spmd.clone, body=%wide.region_4.8_spmd.clone.sunk | while | flops 289298944 | bytes 34494916 | solution.py:160
  221.6 14.0 all_to_all.55
  238.5 6.1 fusion.64
  244.6 24.8 %all-gather.15.cloned.1.call-done = bf16[1024,4096]{1,0:T(8,128)(2,1)} async-done(((bf16[128,4096]{1,0:T(8,128)(2,1)}), bf16[1024,4096]{1,0:T(8,128)(2,1)}) %all-gather.15.cloned.1.call-update) | async-done | bytes 8388624 | tf_op jit(solution)/shard_map/all_gather | solution.py:73
  269.4 6.0 fusion.65
  275.4 50.2 %all-gather.17.cloned.1.call-done = bf16[4096,1024]{1,0:T(8,128)(2,1)} async-done(((bf16[512,1024]{1,0:T(8,128)(2,1)}), bf16[4096,1024]{1,0:T(8,128)(2,1)}) %all-gather.17.cloned.1.call-update) | async-done | bytes 8388624 | tf_op jit(solution)/shard_map/all_gather | solution.py:74
  325.6 9.0 multiply_convert_fusion
  334.6 7.1 fusion.66
  346.6 4.6 all-to-all-start.2
  351.5 9.1 all-to-all-done.2
  362.6 124.2 %while.38 = (s32[]{:T(128)}, f32[512,4,64]{0,2,1:T(8,128)}, f32[4,2]{0,1:T(2,128)S(1)}, bf16[8,512,2,256]{3,1,0,2:T(8,128)(2,1)}, s32[8]{0:T(128)S(1)}, /*index=...) while((s32[]{:T(128)}, f32[512,4,64]{0,2,1:T(8,128)}, ...), condition=%wide.region_16.17_spmd.clone, body=%wide.region_12.16_spmd.clone.sunk | while | flops 693514752 | bytes 30194844 | solution.py:241
  367.0 4.2 fusion.149
  397.2 4.2 fusion.149
  412.8 4.2 fusion.149
  491.0 45.4 %reduce-scatter.7.cloned.1.call-done = bf16[512,2,256]{2,0,1:T(8,128)(2,1)} async-done(((bf16[4096,2,256]{2,0,1:T(8,128)(2,1)}), bf16[512,2,256]{2,0,1:T(8,128)(2,1)}) %reduce-scatter.7.cloned.1.call-update) | async-done | bytes 524304 | tf_op jit(solution)/shard_map/reduce_scatter | solution.py:245
  538.2 33.8 %all_to_all.56 = bf16[512,3,1,256]{3,1,2,0:T(4,128)(2,1)S(1)} all-to-all(bf16[512,3,1,256]{3,1,2,0:T(4,128)(2,1)S(1)} %copy.99), channel_id=1, replica_groups=mesh['seq'=4,'fsdp'=8] {'seq'}, dimensions={0} | all-to-all | bytes 1572864 | tf_op jit(solution)/shard_map/all_to_all | solution.py:253
  576.3 6.4 fusion.55
  584.0 8.1 fusion.67
  593.3 8.1 fusion.68
  602.7 8.1 fusion.69
  611.8 5.5 fusion.35
  617.4 5.1 fusion.40
  622.5 38.8 %all-reduce.8 = (f32[1024]{0:T(1024)S(1)}, f32[1024]{0:T(1024)S(1)}, f32[64]{0:T(128)}, f32[64]{0:T(128)}, f32[16,2]{0,1:T(2,128)}) all-reduce(f32[1024]{0:T(1024)S(1)} %get-tuple-element.567, f32[1024]{0:T(1024)S(1)} %get-tuple-element.565, f32[64]{0:T(128)S(1)} %get-tuple-element.562, ...), channel_id=8, replica_groups=mesh['seq'=4,'fsdp'=8] {'seq','fsdp'}, use_global_device_ids=true, to_apply=%region_27.28.clone | all-reduce | flops 2208 | bytes 17664
  663.5 18.5 %reduce-scatter.11.cloned.1.call-done = f32[32,1024]{1,0:T(8,128)} async-done(((f32[1024,1024]{1,0:T(8,128)}), f32[32,1024]{1,0:T(8,128)}) %reduce-scatter.11.cloned.1.call-update) | async-done | bytes 131088 | tf_op jit(solution)/shard_map/reduce_scatter | solution.py:269
  682.0 159.7 %reduce-scatter.9.cloned.1.call-done = f32[32,3072]{1,0:T(8,128)} async-done(((f32[1024,3072]{1,0:T(8,128)}), f32[32,3072]{1,0:T(8,128)}) %reduce-scatter.9.cloned.1.call-update) | async-done | bytes 393232 | tf_op jit(solution)/shard_map/reduce_scatter | solution.py:268
  841.7 184.6 %reduce-scatter.13.cloned.1.call-done = f32[32,4096]{1,0:T(8,128)} async-done(((f32[1024,4096]{1,0:T(8,128)}), f32[32,4096]{1,0:T(8,128)}) %reduce-scatter.13.cloned.1.call-update) | async-done | bytes 524304 | tf_op jit(solution)/shard_map/reduce_scatter | solution.py:270
  1026.3 187.4 %reduce-scatter.15.cloned.1.call-done = f32[32,4096]{1,0:T(8,128)} async-done(((f32[1024,4096]{1,0:T(8,128)}), f32[32,4096]{1,0:T(8,128)}) %reduce-scatter.15.cloned.1.call-update) | async-done | bytes 524304 | tf_op jit(solution)/shard_map/reduce_scatter | solution.py:271
  1213.7 187.2 %reduce-scatter.17.cloned.1.call-done = f32[128,1024]{1,0:T(8,128)} async-done(((f32[4096,1024]{1,0:T(8,128)}), f32[128,1024]{1,0:T(8,128)}) %reduce-scatter.17.cloned.1.call-update) | async-done | bytes 524304 | tf_op jit(solution)/shard_map/reduce_scatter | solution.py:272
  (454 shorter events, 236.2 us)
Async XLA Ops:
  7.2 87.7 %copy-start = (f32[16,2]{0,1:T(2,128)S(1)}, f32[16,2]{0,1:T(2,128)}, u32[]{:S(2)}) copy-start(f32[16,2]{0,1:T(2,128)} %param.28) | copy-start | bytes 388
  7.2 51.0 %all-gather.7.cloned.1.call-start = ((), (), s32[]{:S(2)}) async-start(), calls=%async_computation.10 | async-start | bytes 7077888 | tf_op jit(solution)/shard_map/all_gather | solution.py:70
  7.9 119.3 %all-gather.9.cloned.1.call-start = ((), (), s32[]{:S(2)}) async-start(), calls=%async_computation.11 | async-start | bytes 4718592 | tf_op jit(solution)/shard_map/all_gather | solution.py:153
  10.6 53.3 %copy-start.30 = (f32[64]{0:T(128)S(1)}, f32[64]{0:T(128)}, u32[]{:S(2)}) copy-start(f32[64]{0:T(128)} %param.26) | copy-start | bytes 772
  10.6 53.3 %copy-start.31 = (f32[64]{0:T(128)S(1)}, f32[64]{0:T(128)}, u32[]{:S(2)}) copy-start(f32[64]{0:T(128)} %param.27) | copy-start | bytes 772
  91.5 144.5 %all-gather.11.cloned.1.call-start = ((), (), s32[]{:S(2)}) async-start(), calls=%async_computation.12 | async-start | bytes 2359296 | tf_op jit(solution)/shard_map/all_gather | solution.py:71
  92.3 146.2 %all-gather.13.cloned.1.call-start = ((), (), s32[]{:S(2)}) async-start(), calls=%async_computation.13 | async-start | bytes 9437184 | tf_op jit(solution)/shard_map/all_gather | solution.py:72
  92.8 176.6 %all-gather.15.cloned.1.call-start = ((), (), s32[]{:S(2)}) async-start(), calls=%async_computation.14 | async-start | bytes 9437184 | tf_op jit(solution)/shard_map/all_gather | solution.py:73
  93.4 232.2 %all-gather.17.cloned.1.call-start = ((), (), s32[]{:S(2)}) async-start(), calls=%async_computation.15 | async-start | bytes 9437184 | tf_op jit(solution)/shard_map/all_gather | solution.py:74
  219.9 16.1 %copy-start.11 = (bf16[128,1024]{1,0:T(8,128)(2,1)S(1)}, bf16[128,1024]{1,0:T(8,128)(2,1)}, u32[]{:S(2)}) copy-start(bf16[128,1024]{1,0:T(8,128)(2,1)} %param.19) | copy-start | bytes 786436
  220.0 18.4 %copy-start.29 = (f32[1024]{0:T(1024)S(1)}, f32[1024]{0:T(1024)}, u32[]{:S(2)}) copy-start(f32[1024]{0:T(1024)} %param.30) | copy-start | bytes 12292
  236.0 8.6 copy-start.23
  238.3 106.5 %copy-start.9 = (f32[128,1024]{1,0:T(8,128)}, f32[128,1024]{1,0:T(8,128)S(1)}, u32[]{:S(2)}) copy-start(f32[128,1024]{1,0:T(8,128)S(1)} %get-tuple-element.667) | copy-start | bytes 1572868
  238.4 31.0 %copy-start.13 = (bf16[128,1024]{1,0:T(8,128)(2,1)}, bf16[128,1024]{1,0:T(8,128)(2,1)S(1)}, u32[]{:S(2)}) copy-start(bf16[128,1024]{1,0:T(8,128)(2,1)S(1)} %multiply_convert_fusion.2) | copy-start | bytes 786436
  244.6 81.0 %copy-start.25 = (bf16[128,1024]{1,0:T(8,128)(2,1)S(1)}, bf16[128,1024]{1,0:T(8,128)(2,1)}, u32[]{:S(2)}) copy-start(bf16[128,1024]{1,0:T(8,128)(2,1)} %param.20) | copy-start | bytes 786436
  345.0 17.6 %copy-start.16 = (f32[128,1024]{1,0:T(8,128)}, f32[128,1024]{1,0:T(8,128)S(1)}, u32[]{:S(2)}) copy-start(f32[128,1024]{1,0:T(8,128)S(1)} %fusion.41) | copy-start | bytes 1572868
  346.6 13.9 all-to-all-start.2
  351.2 185.2 %reduce-scatter.7.cloned.1.call-start = ((), (), s32[]{:S(2)}) async-start(), calls=%async_computation.16 | async-start | bytes 4718592 | tf_op jit(solution)/shard_map/reduce_scatter | solution.py:245
  362.6 8.5 copy-start.4
  377.2 8.5 copy-start.4
  392.9 8.5 copy-start.4
  408.5 8.5 copy-start.4
  439.8 8.5 copy-start.4
  455.5 8.5 copy-start.4
  471.1 8.5 copy-start.4
  486.8 195.2 %reduce-scatter.11.cloned.1.call-start = ((), (), s32[]{:S(2)}) async-start(), calls=%async_computation.18 | async-start | bytes 4325376 | tf_op jit(solution)/shard_map/reduce_scatter | solution.py:269
  490.7 350.9 %reduce-scatter.9.cloned.1.call-start = ((), (), s32[]{:S(2)}) async-start(), calls=%async_computation.17 | async-start | bytes 12976128 | tf_op jit(solution)/shard_map/reduce_scatter | solution.py:268
  582.7 443.6 %reduce-scatter.13.cloned.1.call-start = ((), (), s32[]{:S(2)}) async-start(), calls=%async_computation.19 | async-start | bytes 17301504 | tf_op jit(solution)/shard_map/reduce_scatter | solution.py:270
  592.1 621.6 %reduce-scatter.15.cloned.1.call-start = ((), (), s32[]{:S(2)}) async-start(), calls=%async_computation.20 | async-start | bytes 17301504 | tf_op jit(solution)/shard_map/reduce_scatter | solution.py:271
  601.4 799.5 %reduce-scatter.17.cloned.1.call-start = ((), (), s32[]{:S(2)}) async-start(), calls=%async_computation.21 | async-start | bytes 17301504 | tf_op jit(solution)/shard_map/reduce_scatter | solution.py:272
  617.3 45.2 %copy-start.33 = (f32[128]{0:T(128)S(1)}, f32[128]{0:T(128)}, u32[]{:S(2)}) copy-start(f32[128]{0:T(128)} %copy-done.32) | copy-start | bytes 1540
  617.3 783.6 %copy-start.1 = (f32[16,2]{0,1:T(2,128)S(1)}, f32[16,2]{0,1:T(2,128)}, u32[]{:S(2)}) copy-start(f32[16,2]{0,1:T(2,128)} %param.28) | copy-start | bytes 388
  (36 other events, 112.2 us)
Sparse Core Ops, SparseCore 0:
  9.9 48.2 all-gather.6
  91.6 35.5 all-gather.8
  129.1 27.9 all-gather.10
  158.8 54.3 all-gather.12
  215.0 54.3 all-gather.14
  271.2 54.3 all-gather.16
  486.9 49.4 reduce-scatter.6
  539.3 142.6 reduce-scatter.10
  689.6 151.9 reduce-scatter.8
  844.4 181.8 reduce-scatter.12
  1029.2 184.5 reduce-scatter.14
  1216.5 184.3 reduce-scatter.16
where the time goes:
time: 1420 us; the launch traced here: 1410 us
  waiting for transfers between devices  950 us (67%)
  matrix products  213 us (15%)
  blocking collectives  112 us (8%)
  local copies, waits for them, and re-layouts  59.7 us (4%)
  other arithmetic  47.2 us (3%)
  between operations  15.3 us (1%)
    reduce_scatter x1, waiting for transfers between devices, per_device(): lax.psum_scatter(up_grad, ('seq', 'fsdp'), scatter_dimension=0, tiled=True)  187 us
    reduce_scatter x1, waiting for transfers between devices, per_device(): lax.psum_scatter(down_grad, ('seq', 'fsdp'), scatter_dimension=0, tiled=T...  187 us
    reduce_scatter x1, waiting for transfers between devices, per_device(): lax.psum_scatter(gate_grad, ('seq', 'fsdp'), scatter_dimension=0, tiled=T...  185 us
    reduce_scatter x1, waiting for transfers between devices, per_device(): lax.psum_scatter(attn_grad, ('seq', 'fsdp'), scatter_dimension=0, tiled=T...  160 us
    all_gather x1, waiting for transfers between devices, per_device(): lax.all_gather(w_down, 'fsdp', axis=0, tiled=True)  50.2 us
    all_gather x1, waiting for transfers between devices, per_device(): lax.all_gather(w_attn, 'fsdp', axis=0, tiled=True)  47.6 us
    reduce_scatter x1, waiting for transfers between devices, per_device(): lax.psum_scatter(kv_grads.astype(jnp.bfloat16), 'fsdp', scatter_dimension...  45.4 us
    unnamed x1, blocking collectives  38.8 us
  transfers between devices with their start and end apart: 13, of which 11 were waited for; matrix products, arithmetic and copies ran while one was open for 12% of the time, Pallas kernels for 0%

commit v1 on v0

v1 whole, which is shorter than its diff:
```python
import functools

import jax
import jax.numpy as jnp
from jax import lax
from jax.experimental import pallas as pl
from jax.experimental.pallas import tpu as pltpu
from jax.sharding import PartitionSpec as P

EPSILON = 1e-06
F32, BF16 = jnp.float32, jnp.bfloat16
VARIATES = 8
AWAY = 1024.0
QUERY_BLOCK = 256
LSE_ROW, VAR_ROW = 32, 40
MESH = pl.DeviceIdType.MESH
ANY = pl.BlockSpec(memory_space=pl.ANY)
VMEM = pl.BlockSpec(memory_space=pltpu.VMEM)
VMEM_BYTES = 48 * 2**20


def nn(a, b):
    return jnp.dot(a, b, preferred_element_type=F32)


def nt(a, b):
    return lax.dot_general(a, b, (((1,), (1,)), ((), ())), preferred_element_type=F32)


def tn(a, b):
    return lax.dot_general(a, b, (((0,), (0,)), ((), ())), preferred_element_type=F32)


def pieces(values):
    high = values.astype(BF16).astype(F32)
    middle = (values - high).astype(BF16).astype(F32)
    return high, middle, (values - high - middle).astype(BF16).astype(F32)


def send_all(plan, send_sems, recv_sems, local_sems):
    remote, local = plan
    copies = []
    for n, (src, dst, device, may_send, may_receive) in enumerate(remote):
        copy = pltpu.make_async_remote_copy(
            src_ref=src,
            dst_ref=dst,
            send_sem=send_sems.at[n],
            recv_sem=recv_sems.at[n],
            device_id=device,
            device_id_type=MESH,
        )
        when(may_send, copy.start)
        copies.append((copy, may_send, may_receive))
    locals_ = []
    for n, (src, dst, may) in enumerate(local):
        copy = pltpu.make_async_copy(src, dst, local_sems.at[n])
        when(may, copy.start)
        locals_.append((copy, may))

    def finish():
        for copy, may in locals_:
            when(may, copy.wait)
        for copy, may_send, may_receive in copies:
            when(may_send, copy.wait_send)
            when(may_receive, copy.wait_recv)

    return finish


def when(condition, action):
    if condition is None:
        action()
    else:
        pl.when(condition)(action)


def greet(devices):
    barrier = pltpu.get_barrier_semaphore()
    for device in devices:
        pl.semaphore_signal(barrier, inc=1, device_id=device, device_id_type=MESH)
    pl.semaphore_wait(barrier, len(devices))


def exchange(number, inputs, out_shapes, make_plan, peers, counts):
    def kernel(*refs):
        ins = refs[: len(inputs)]
        outs = refs[len(inputs) : len(inputs) + len(out_shapes)]
        send_sems, recv_sems, local_sems = refs[-3:]
        s, f = lax.axis_index("seq"), lax.axis_index("fsdp")
        greet(peers(s, f))
        send_all(make_plan(s, f, ins, outs), send_sems, recv_sems, local_sems)()

    return pl.pallas_call(
        kernel,
        in_specs=[ANY] * len(inputs),
        out_specs=[ANY] * len(out_shapes),
        out_shape=out_shapes,
        scratch_shapes=[
            pltpu.SemaphoreType.DMA((counts[0],)),
            pltpu.SemaphoreType.DMA((counts[0],)),
            pltpu.SemaphoreType.DMA((max(counts[1], 1),)),
        ],
        compiler_params=pltpu.CompilerParams(collective_id=number, has_side_effects=True),
    )(*inputs)


def shape(dims, dtype=BF16):
    return jax.ShapeDtypeStruct(tuple(dims), dtype)


def join(a, b):
    return jnp.concatenate([a, b], axis=0)


def forward_kernel(q_ref, kv_ref, qa_ref, ka_ref, o_ref, att_ref, lse_ref):
    width, rows = q_ref.shape[1:]
    blocks = rows // QUERY_BLOCK

    def block(i, _):
        j = i // blocks
        cols = pl.ds(pl.multiple_of((i % blocks) * QUERY_BLOCK, QUERY_BLOCK), QUERY_BLOCK)
        queries = join(q_ref[j, :, cols], qa_ref[j, :, cols]).T
        total = jnp.zeros((QUERY_BLOCK, 2 * width), F32)
        for g in range(kv_ref.shape[0]):
            keys = join(kv_ref[g, :width, :], ka_ref[g])
            values = join(kv_ref[g, width:, :], jnp.ones((width, rows), BF16))
            weights = jnp.exp(nn(queries, keys)).astype(BF16)
            total += nt(weights, values)
        total = total.T
        weight_sum = total[width : width + 1]
        attended = total[:width] / weight_sum
        att_ref[j, :, cols] = attended
        o_ref[j, :, cols] = attended.astype(BF16)
        lse_ref[j, :, cols] = jnp.log(weight_sum)
        return 0

    lax.fori_loop(0, q_ref.shape[0] * blocks, block, 0)


def attention_forward(q, kv, qa, ka):
    groups, width, rows = q.shape
    return pl.pallas_call(
        forward_kernel,
        in_specs=[VMEM] * 4,
        out_specs=[VMEM] * 3,
        out_shape=[shape(q.shape), shape(q.shape, F32), shape((groups, 1, rows), F32)],
        compiler_params=pltpu.CompilerParams(vmem_limit_bytes=VMEM_BYTES),
        cost_estimate=pl.CostEstimate(
            flops=groups * rows * kv.shape[0] * rows * 8 * width,
            bytes_accessed=8 * 2**20,
            transcendentals=groups * rows * kv.shape[0] * rows,
        ),
    )(q, kv, qa, ka)


def with_rows(base, first, rows):
    index = lax.broadcasted_iota(jnp.int32, base.shape, 0)
    for n, row in enumerate(rows):
        base = jnp.where(index == first + n, row, base)
    return base


def backward_body(q_ref, kv_ref, qa_ref, ka_ref, do_ref, att_ref, lse_ref, dq_ref, dkv_ref, bias_ref, sum_ref):
    width, rows = q_ref.shape[1:]
    blocks = rows // QUERY_BLOCK
    parts = do_ref.shape[1]
    span = rows // parts
    sum_ref[...] = jnp.zeros_like(sum_ref)
    bias_ref[...] = jnp.zeros_like(bias_ref)

    def block(i, _):
        j = i // blocks
        first = (i % blocks) * QUERY_BLOCK
        cols = pl.ds(pl.multiple_of(first, QUERY_BLOCK), QUERY_BLOCK)
        q_t = q_ref[j, :, cols]
        marks = qa_ref[j, :, cols].astype(F32)
        extra = with_rows(marks, LSE_ROW, pieces(-lse_ref[j, :, cols])).astype(BF16)
        queries = join(q_t, extra).T
        grad_t = jnp.concatenate(
            [do_ref[j, first // span + n] for n in range(QUERY_BLOCK // span)], axis=1
        )
        delta = jnp.sum(grad_t.astype(F32) * att_ref[j, :, cols], axis=0, keepdims=True)
        extra = with_rows(jnp.zeros((width, QUERY_BLOCK), F32), 0, pieces(-delta)).astype(BF16)
        grads = join(grad_t, extra).T
        query_sum = jnp.zeros((QUERY_BLOCK, 2 * width), F32)
        for g in range(kv_ref.shape[0]):
            keys = join(kv_ref[g, :width, :], ka_ref[g])
            values = join(kv_ref[g, width:, :], jnp.ones((width, rows), BF16))
            probs = jnp.exp(nn(queries, keys))
            score_grad = (probs * nn(grads, values)).astype(BF16)
            sum_ref[g, width:, :] += nn(grad_t, probs.astype(BF16))
            sum_ref[g, :width, :] += nn(q_t, score_grad)
            query_sum += nt(score_grad, keys)
        query_sum = query_sum.T
        dq_ref[j, :, cols] = (query_sum[:width] * width**-0.5).astype(BF16)
        by_variate = query_sum[width : width + VARIATES]
        bias_ref[0] += by_variate * marks[VAR_ROW : VAR_ROW + VARIATES]
        bias_ref[1] += by_variate
        return 0

    lax.fori_loop(0, q_ref.shape[0] * blocks, block, 0)
    dkv_ref[...] = sum_ref[...].astype(BF16)


def rms_scale(vector, gain, axis=-1):
    return vector * lax.rsqrt(jnp.mean(vector * vector, axis=axis, keepdims=True) + EPSILON) * gain


def norm_back(grad, vector, gain):
    inverse = lax.rsqrt(jnp.mean(vector * vector, axis=-1, keepdims=True) + EPSILON)
    scaled = grad * gain
    mean = jnp.mean(scaled * vector, axis=-1, keepdims=True)
    return inverse * scaled - vector * (inverse**3 * mean), jnp.sum(grad * vector * inverse, axis=0)


def per_device(
    tokens,
    cotangent,
    doc_starts,
    variate_ids,
    time_ids,
    gain_attn,
    w_attn,
    gain_query,
    gain_key,
    variate_bias,
    w_output,
    gain_feed,
    w_gate,
    w_up,
    w_down,
):
    S, F = lax.axis_size("seq"), lax.axis_size("fsdp")
    s, f = lax.axis_index("seq"), lax.axis_index("fsdp")
    rows, width = tokens.shape
    heads = variate_bias.shape[0]
    dim = gain_query.shape[0]
    own_heads = heads // S
    splits = F // own_heads
    group = rows * S
    groups = F // splits
    hidden = w_down.shape[0] * F // S
    half = F // 2
    cut = width // (S * F)
    lanes = own_heads * dim

    def along_seq(s, f):
        return [(lax.rem(s + d, S), f) for d in range(1, S)]

    def along_fsdp(s, f):
        return [(s, lax.rem(f + d, F)) for d in range(1, F)]

    def along_both(s, f):
        return along_seq(s, f) + along_fsdp(s, f)

    def like_parts(s, f):
        return [
            (lax.rem(s + a, S), lax.rem(f + b * splits, F))
            for a in range(S)
            for b in range(groups)
            if a or b
        ]

    def everyone(s, f):
        return [(lax.rem(s + a, S), lax.rem(f + b, F)) for a in range(S) for b in range(F) if a or b]

    def seq_swap(s, f, src, dst):
        remote = [(src.at[t[0]], dst.at[s], t, None, None) for t in along_seq(s, f)]
        return remote, [(src.at[s], dst.at[s], None)]

    w_heads = lax.dynamic_slice_in_dim(
        w_attn.reshape(-1, 3, S, lanes), s, 1, 2
    ).reshape(-1, 3 * lanes)
    per_plane = F // S
    down_rows = w_down.shape[0] // S

    def plan_a(s, f, ins, outs):
        x, w, down = ins
        xs, ws, mine = outs
        remote = [(x, xs.at[s], t, None, None) for t in along_seq(s, f)]
        remote += [(w, ws.at[f], t, None, None) for t in along_fsdp(s, f)]
        local = [(x, xs.at[s], None), (w, ws.at[f], None)]
        holds = f // per_plane == s
        source = s * per_plane + f // S
        for i in range(S):
            to = lax.rem(f, per_plane) * S + i
            send = jnp.logical_and(holds, to != f)
            if i == 0:
                get = source != f
            else:
                get = False
            remote.append((down.at[i], mine, (s, to), send, get))
            local.append((down.at[i], mine, jnp.logical_and(holds, to == f)))
        return remote, local

    x_parts, w_parts, down_mine = exchange_a(
        [tokens, w_heads, w_down.reshape(S, down_rows, width)],
        [shape((S, rows, width)), shape((F,) + w_heads.shape), shape((down_rows, width))],
        plan_a,
        along_both,
        (S - 1) + (F - 1),
        S,
    )
    w_qkv = w_parts.reshape(width, 3 * lanes)
    inputs = x_parts.reshape(group, width).astype(F32)

    packed = jnp.concatenate(
        [
            lax.dynamic_slice_in_dim(w_gate, s * hidden, hidden, 1),
            lax.dynamic_slice_in_dim(w_up, s * hidden, hidden, 1),
            w_output,
            down_mine.reshape(w_gate.shape[0], hidden),
        ],
        axis=1,
    )
    gathered = lax.all_gather(packed, "fsdp", axis=0, tiled=True)
    later_cot, _ = lax.optimization_barrier((cotangent, x_parts))
    cot_group = lax.all_gather(later_cot, "seq", axis=0, tiled=True)

    normed = rms_scale(inputs, gain_attn).astype(BF16)
    projected = lax.dot_general(
        w_qkv, normed, (((0,), (1,)), ((), ())), preferred_element_type=F32
    ).reshape(3, own_heads, dim, group)
    times = lax.dynamic_slice_in_dim(time_ids, f * group, group).astype(F32)
    frequency = 10000.0 ** (-2.0 * jnp.arange(dim // 2, dtype=F32) / dim)
    angles = frequency[:, None] * times[None, :]
    cosine, sine = jnp.cos(angles), jnp.sin(angles)

    def prepare(raw, gain):
        front, back = jnp.split(rms_scale(raw, gain[:, None], axis=1), 2, axis=1)
        return jnp.concatenate([front * cosine - back * sine, front * sine + back * cosine], axis=1)

    queries, query_pull = jax.vjp(prepare, projected[0], gain_query)
    key_rows, key_pull = jax.vjp(prepare, projected[1], gain_key)
    queries = queries.astype(BF16) * dim**-0.5
    kv = jnp.concatenate([key_rows, projected[2]], axis=1).astype(BF16)

    def plan_b(s, f, ins, outs):
        q, kv = ins
        qs, kvs = outs
        remote, local = [], [(kv.at[f // splits], kvs.at[f], None), (q.at[f // splits], qs.at[f // splits], None)]
        for d in range(1, F):
            to = lax.rem(f + d, F)
            remote.append((kv.at[to // splits], kvs.at[f], (s, to), None, None))
            if d % splits == 0:
                remote.append((q.at[to // splits], qs.at[f // splits], (s, to), None, None))
        return remote, local

    q_all, kv_all = exchange(
        1,
        [queries, kv],
        [shape((groups, dim, group)), shape((F, 2 * dim, group))],
        plan_b,
        along_fsdp,
        (F - 1 + groups - 1, 2),
    )

    head = s * own_heads + f // splits
    part = lax.rem(f, splits)
    total = F * group
    positions = jnp.arange(total, dtype=jnp.int32)
    docs = jnp.sum((doc_starts[:, None] <= positions[None, :]).astype(jnp.int32), axis=0) - 1
    doc_marks = (docs[None, :] == jnp.arange(doc_starts.shape[0])[:, None]).astype(F32)
    var_marks = (variate_ids[None, :] == jnp.arange(VARIATES)[:, None]).astype(F32)
    nothing = jnp.zeros((dim - LSE_ROW - 3, total), F32)
    key_marks = jnp.concatenate(
        [var_marks, var_marks, var_marks, 1.0 - doc_marks, jnp.ones((3, total), F32), nothing]
    ).astype(BF16)
    key_marks = key_marks.reshape(dim, F, group).transpose(1, 0, 2)
    my_bias = lax.dynamic_slice_in_dim(variate_bias, head, 1, 0)[0]
    high, middle_, low = pieces(my_bias[0] - my_bias[1])

    def mine(marks):
        marks = marks.reshape(-1, groups, splits, group)
        return lax.dynamic_slice_in_dim(marks, part, 1, 2)[:, :, 0]

    var_mine, doc_mine = mine(var_marks), mine(doc_marks)
    query_marks = jnp.concatenate(
        [
            var_mine * high,
            var_mine * middle_,
            var_mine * low,
            doc_mine * -AWAY,
            jnp.zeros((VAR_ROW - LSE_ROW, groups, group), F32),
            var_mine,
            jnp.zeros((dim - VAR_ROW - VARIATES, groups, group), F32),
        ]
    ).astype(BF16)
    query_marks = query_marks.transpose(1, 0, 2)

    attended_low, attended, log_sum = attention_forward(q_all, kv_all, query_marks, key_marks)

    def plan_d(s, f, ins, outs):
        (o,), (all_heads,) = ins, outs
        own = s * own_heads + f // splits
        remote = [
            (o.at[t[1] // splits], all_heads.at[own], t, None, None) for t in like_parts(s, f)
        ]
        return remote, [(o.at[f // splits], all_heads.at[own], None)]

    heads_t = exchange(
        2,
        [attended_low],
        [shape((heads, dim, group))],
        plan_d,
        like_parts,
        (S * groups - 1, 1),
    )[0].reshape(heads * dim, group)

    gate_full, up_full, output_full, down_full = jnp.split(
        gathered, [hidden, 2 * hidden, 2 * hidden + width], axis=1
    )
    down_full = down_full.reshape(hidden, width)
    middle = inputs + tn(heads_t, output_full)
    normed_mid = rms_scale(middle, gain_feed).astype(BF16)
    gate_act, up_act = nn(normed_mid, gate_full), nn(normed_mid, up_full)
    hidden_grad = nt(cot_group, down_full)
    sigmoid = jax.nn.sigmoid(gate_act)
    silu = gate_act * sigmoid
    hidden_low = (silu * up_act).astype(BF16)
    gate_low = (hidden_grad * up_act * sigmoid * (1.0 + gate_act * (1.0 - sigmoid))).astype(BF16)
    up_low = (hidden_grad * silu).astype(BF16)
    mid_part = (nt(gate_low, gate_full) + nt(up_low, up_full)).astype(BF16)
    out_part = nn(hidden_low, down_full).astype(BF16)
    by_owner = (S, half, 2, cut)
    gate_part = tn(normed_mid, gate_low).astype(BF16).reshape(by_owner + (hidden,))
    up_part = tn(normed_mid, up_low).astype(BF16).reshape(by_owner + (hidden,))
    down_part = tn(hidden_low, cot_group).astype(BF16).reshape(half, 2, down_rows, width)

    def pair(s, f):
        return (s, f + 1 - 2 * lax.rem(f, 2))

    def plan_e(s, f, ins, outs):
        u, gate, up, down = ins
        us, gates, ups, downs = outs
        remote, local = seq_swap(s, f, u, us)
        other = 1 - lax.rem(f, 2)
        for src, dst in ((gate.at[:, :, other], gates), (up.at[:, :, other], ups), (down.at[:, other], downs)):
            remote.append((src, dst, pair(s, f), None, None))
        return remote, local

    mid_terms, gate_other, up_other, down_other = exchange(
        3,
        [mid_part.reshape(S, rows, width), gate_part, up_part, down_part],
        [
            shape((S, rows, width)),
            shape((S, half, cut, hidden)),
            shape((S, half, cut, hidden)),
            shape((half, down_rows, width)),
        ],
        plan_e,
        lambda s, f: along_seq(s, f) + [pair(s, f)],
        (S - 1 + 3, 1),
    )
    parity = lax.rem(f, 2)

    def halves(own, other, axis):
        own = lax.dynamic_index_in_dim(own, parity, axis, keepdims=False)
        return (own.astype(F32) + other.astype(F32)).astype(BF16)

    own_middle = lax.dynamic_slice_in_dim(middle, s * rows, rows, 0)
    mid_grad, feed_gain = norm_back(jnp.sum(mid_terms.astype(F32), axis=0), own_middle, gain_feed)
    middle_grad = cotangent.astype(F32) + mid_grad
    middle_low = middle_grad.astype(BF16)
    heads_grad = nt(output_full, middle_low).astype(BF16).reshape(heads, dim, rows)
    own_heads_t = lax.dynamic_slice_in_dim(heads_t, s * rows, rows, 1)
    output_part = nn(own_heads_t, middle_low).astype(BF16).reshape(by_owner + (width,))

    def plan_f(s, f, ins, outs):
        grad, out = ins
        grads, outs_ = outs
        place = grads.at[f // splits, s]
        remote = [
            (grad.at[t[0] * own_heads + t[1] // splits], place, t, None, None)
            for t in like_parts(s, f)
        ]
        remote.append((out.at[:, :, 1 - lax.rem(f, 2)], outs_, pair(s, f), None, None))
        return remote, [(grad.at[s * own_heads + f // splits], place, None)]

    grad_heads, output_other = exchange(
        4,
        [heads_grad, output_part],
        [shape((groups, S, dim, rows)), shape((S, half, cut, width))],
        plan_f,
        lambda s, f: like_parts(s, f) + [pair(s, f)],
        (S * groups - 1 + 1, 1),
    )
    gate_half = halves(gate_part, gate_other, 2)
    up_half = halves(up_part, up_other, 2)
    down_half = halves(down_part, down_other, 1)
    output_half = halves(output_part, output_other, 2)

    def same_parity(s, f):
        return [(s, lax.rem(f + 2 * d, F)) for d in range(1, half)]

    def kernel_g(*refs):
        ins, sends, outs, gots = refs[:7], refs[7:12], refs[12:15], refs[15:20]
        sum_ref, send_sems, recv_sems, local_sems = refs[20:]
        s, f = lax.axis_index("seq"), lax.axis_index("fsdp")
        greet(along_seq(s, f) + same_parity(s, f))
        remote, local = seq_swap(s, f, sends[4], gots[4])
        for src, dst in zip(sends[:3], gots[:3]):
            for t in same_parity(s, f):
                remote.append((src.at[:, t[1] // 2], dst.at[f // 2], t, None, None))
            local.append((src.at[:, f // 2], dst.at[f // 2], None))
        for t in same_parity(s, f):
            remote.append((sends[3].at[t[1] // 2], gots[3].at[f // 2], t, None, None))
        local.append((sends[3].at[f // 2], gots[3].at[f // 2], None))
        finish = send_all((remote, local), send_sems, recv_sems, local_sems)
        backward_body(*ins, *outs, sum_ref)
        finish()

    copies = S - 1 + 4 * (half - 1)
    owned = (half, S, cut)
    query_grad, kv_grad, bias_terms, gate_got, up_got, output_got, down_got, out_terms = pl.pallas_call(
        kernel_g,
        in_specs=[VMEM] * 7 + [ANY] * 5,
        out_specs=[VMEM] * 3 + [ANY] * 5,
        out_shape=[
            shape(q_all.shape),
            shape(kv_all.shape),
            shape((2, VARIATES, QUERY_BLOCK), F32),
            shape(owned + (hidden,)),
            shape(owned + (hidden,)),
            shape(owned + (width,)),
            shape((half, down_rows, width)),
            shape((S, rows, width)),
        ],
        scratch_shapes=[
            pltpu.VMEM(kv_all.shape, F32),
            pltpu.SemaphoreType.DMA((copies,)),
            pltpu.SemaphoreType.DMA((copies,)),
            pltpu.SemaphoreType.DMA((5,)),
        ],
        compiler_params=pltpu.CompilerParams(
            collective_id=5, has_side_effects=True, vmem_limit_bytes=VMEM_BYTES
        ),
    )(
        q_all,
        kv_all,
        query_marks,
        key_marks,
        grad_heads,
        attended,
        log_sum,
        gate_half,
        up_half,
        output_half,
        down_half,
        out_part.reshape(S, rows, width),
    )
    layer_out = (own_middle + jnp.sum(out_terms.astype(F32), axis=0)).astype(BF16)
    down_grad = jnp.sum(down_got.astype(F32), axis=0)

    def over_pairs(got):
        return jnp.sum(got.astype(F32), axis=0).astype(BF16)

    def plan_h(s, f, ins, outs):
        dq, dkv, *sums = ins
        dqs, dkvs, *gots = outs
        own = f // splits
        remote, local = [], [(dkv.at[f], dkvs.at[f], None), (dq.at[own], dqs.at[own], None)]
        for d in range(1, F):
            to = lax.rem(f + d, F)
            remote.append((dkv.at[to], dkvs.at[f], (s, to), None, None))
            if d % splits == 0:
                remote.append((dq.at[to // splits], dqs.at[own], (s, to), None, None))
        for src, dst in zip(sums, gots):
            more, also = seq_swap(s, f, src, dst)
            remote += more
            local += also
        return remote, local

    wide = shape((S, cut, hidden))
    query_got, kv_got, gate_rows, up_rows, output_rows = exchange(
        6,
        [query_grad, kv_grad, over_pairs(gate_got), over_pairs(up_got), over_pairs(output_got)],
        [shape((own_heads, dim, group)), shape((F, 2 * dim, group)), wide, wide, shape((S, cut, width))],
        plan_h,
        along_both,
        (F - 1 + groups - 1 + 3 * (S - 1), 5),
    )
    gate_grad = gate_rows.astype(F32).transpose(1, 0, 2).reshape(cut, S * hidden)
    up_grad = up_rows.astype(F32).transpose(1, 0, 2).reshape(cut, S * hidden)
    output_grad = jnp.sum(output_rows.astype(F32), axis=0)

    kv_sum = jnp.sum(kv_got.astype(F32).reshape(own_heads, splits, 2 * dim, group), axis=1)
    kv_low = kv_sum.astype(BF16).astype(F32)
    query_raw, query_gain = query_pull(query_got.astype(F32))
    key_raw, key_gain = key_pull(kv_low[:, :dim])
    projected_grad = (
        jnp.stack([query_raw, key_raw, kv_low[:, dim:]]).astype(BF16).reshape(3 * lanes, group)
    )
    normed_part = lax.dot_general(
        projected_grad, w_qkv, (((0,), (1,)), ((), ())), preferred_element_type=F32
    ).astype(BF16)
    attn_part = lax.dot_general(
        normed, projected_grad, (((0,), (1,)), ((), ())), preferred_element_type=F32
    ).astype(BF16)

    def plan_i(s, f, ins, outs):
        u, w = ins
        us, ws = outs
        remote, local = seq_swap(s, f, u, us)
        for t in along_fsdp(s, f):
            remote.append((w.at[:, t[1]], ws.at[f], t, None, None))
        local.append((w.at[:, f], ws.at[f], None))
        return remote, local

    normed_terms, attn_got = exchange(
        7,
        [normed_part.reshape(S, rows, width), attn_part.reshape(S, F, cut, 3 * lanes)],
        [shape((S, rows, width)), shape((F, S, cut, 3 * lanes))],
        plan_i,
        along_both,
        (S - 1 + F - 1, 2),
    )
    input_grad, attn_gain = norm_back(
        jnp.sum(normed_terms.astype(F32), axis=0), tokens.astype(F32), gain_attn
    )
    tokens_grad = middle_grad + input_grad

    bias_sums = jnp.sum(bias_terms, axis=(1, 2))
    bias_pair = jnp.stack([bias_sums[0], bias_sums[1] - bias_sums[0]])
    bias_full = lax.dynamic_update_slice_in_dim(
        jnp.zeros((heads, 2), F32), bias_pair[None], head, 0
    )
    count = S * F
    small = jnp.zeros((count, 8, 128), F32)
    small = small.at[:, 0, :cut].set(attn_gain.reshape(count, cut))
    small = small.at[:, 1, :cut].set(feed_gain.reshape(count, cut))
    small = small.at[:, 2, :dim].set(query_gain)
    small = small.at[:, 3, :dim].set(key_gain)
    small = small.at[:, 4, : 2 * heads].set(bias_full.reshape(-1))

    def plan_j(s, f, ins, outs):
        w, vectors = ins
        ws, got = outs
        remote, local = seq_swap(s, f, w, ws)
        own = s * F + f
        remote += [(vectors.at[t[0] * F + t[1]], got.at[own], t, None, None) for t in everyone(s, f)]
        local.append((vectors.at[own], got.at[own], None))
        return remote, local

    attn_rows, small_got = exchange(
        8,
        [over_pairs(attn_got), small],
        [shape((S, cut, 3 * lanes)), shape((count, 8, 128), F32)],
        plan_j,
        everyone,
        (S - 1 + count - 1, 2),
    )
    attn_grad = (
        attn_rows.astype(F32).reshape(S, cut, 3, lanes).transpose(1, 2, 0, 3).reshape(cut, 3 * heads * dim)
    )
    sums = jnp.sum(small_got, axis=0)
    return (
        layer_out,
        tokens_grad,
        attn_grad,
        output_grad,
        gate_grad,
        up_grad,
        down_grad,
        sums[0, :cut],
        sums[1, :cut],
        sums[2, :dim],
        sums[3, :dim],
        sums[4, : 2 * heads].reshape(heads, 2),
    )


def exchange_a(inputs, out_shapes, make_plan, peers, plain, conditional):
    def kernel(*refs):
        ins, outs = refs[: len(inputs)], refs[len(inputs) : len(inputs) + len(out_shapes)]
        send_sems, recv_sems, local_sems = refs[-3:]
        s, f = lax.axis_index("seq"), lax.axis_index("fsdp")
        greet(peers(s, f))
        remote, local = make_plan(s, f, ins, outs)
        finish = send_all((remote[:plain], local), send_sems, recv_sems, local_sems)
        copies = []
        for n, (src, dst, device, may_send, may_receive) in enumerate(remote[plain:]):
            copy = pltpu.make_async_remote_copy(
                src_ref=src,
                dst_ref=dst,
                send_sem=send_sems.at[plain + n],
                recv_sem=recv_sems.at[plain],
                device_id=device,
                device_id_type=MESH,
            )
            when(may_send, copy.start)
            copies.append((copy, may_send))
        finish()
        for copy, may_send in copies:
            when(may_send, copy.wait_send)
        when(remote[plain][4], copies[0][0].wait_recv)

    return pl.pallas_call(
        kernel,
        in_specs=[ANY] * len(inputs),
        out_specs=[ANY] * len(out_shapes),
        out_shape=out_shapes,
        scratch_shapes=[
            pltpu.SemaphoreType.DMA((plain + conditional,)),
            pltpu.SemaphoreType.DMA((plain + 1,)),
            pltpu.SemaphoreType.DMA((2 + conditional,)),
        ],
        compiler_params=pltpu.CompilerParams(collective_id=0, has_side_effects=True),
    )(*inputs)


def solution(mesh):
    by_token, by_fsdp, by_owner = P(("fsdp", "seq"), None), P("fsdp", None), P(("seq", "fsdp"), None)
    in_specs = (
        by_token,
        by_token,
        P(),
        P(),
        P(),
        P(),
        by_fsdp,
        P(),
        P(),
        P(),
        by_fsdp,
        P(),
        by_fsdp,
        by_fsdp,
        by_fsdp,
    )
    out_specs = (
        (by_token, by_token) + (by_owner,) * 5 + (P(("seq", "fsdp")),) * 2 + (P(),) * 3
    )
    return jax.shard_map(
        per_device, mesh=mesh, in_specs=in_specs, out_specs=out_specs, check_vma=False
    )
```

time: 1420 us -> 389 us (0.27)
  waiting for transfers between devices: 950 us -> 23.8 us
  Pallas kernels: 0 us -> 243 us
  matrix products: 213 us -> 41.5 us
  blocking collectives: 112 us -> 0 us
  local copies, waits for them, and re-layouts: 59.7 us -> 23.1 us
    reduce_scatter x6 -> x0, waiting for transfers between devices: 783 us -> none  [the longest x1 187 us: per_device(): lax.psum_scatter(up_grad, ('seq', 'fsdp'), scatter_dimension=0, tiled=True)]
    pallas_call x0 -> x10, Pallas kernels: none -> 243 us  [the longest x7 147 us: exchange(): pl.pallas_call(kernel, in_specs=[ANY] * len(inputs), out_specs=[ANY] * le...]
    dot_general x71 -> x15, matrix products: 213 us -> 41.5 us  [the longest x4 14.9 us: nn(): return jnp.dot(a, b, preferred_element_type=F32)]
    all_gather x6 -> x2, waiting for transfers between devices: 155 us -> 23 us  [the longest x1 19.4 us: per_device(): cot_group = lax.all_gather(later_cot, 'seq', axis=0, tiled=True)]
    all_to_all x3 -> x0, blocking collectives: 72.7 us -> none  [the longest x1 33.8 us: per_device(): lax.all_to_all(head_grads, 'seq', split_axis=0, concat_axis=2, tiled=True)]
    unnamed x1 -> x0, blocking collectives: 38.8 us -> none
    reduce_sum x29 -> x22, other arithmetic: 34.8 us -> 13.2 us  [the longest x4 4.99 us: over_pairs(): return jnp.sum(got.astype(F32), axis=0).astype(BF16)]
    dynamic_slice x26 -> x6, local copies, waits for them, and re-layouts: 17.8 us -> 1.11 us  [the longest x1 0.98 us: per_device(): lax.dynamic_slice_in_dim(w_gate, s * hidden, hidden, 1)]
  transfers between devices with their start and end apart: 13 -> 2, of which waited for: 11 -> 2; matrix products, arithmetic and copies ran while one was open for 12% -> 4% of each run, Pallas kernels for 0% -> 16%
where the time goes in v1:
time: 389 us; the launch traced here: 384 us
  Pallas kernels  243 us (62%)
  matrix products  41.5 us (11%)
  other arithmetic  34.3 us (9%)
  waiting for transfers between devices  23.8 us (6%)
  local copies, waits for them, and re-layouts  23.1 us (6%)
  between operations  18 us (5%)
    pallas_call x7, Pallas kernels, exchange(): pl.pallas_call(kernel, in_specs=[ANY] * len(inputs), out_specs=[ANY] * le...  147 us
    pallas_call x1, Pallas kernels, per_device(): pl.pallas_call(kernel_g, in_specs=[VMEM] * 7 + [ANY] * 5, out_specs=[VMEM...  49.8 us
    pallas_call x1, Pallas kernels, exchange_a(): pl.pallas_call(kernel, in_specs=[ANY] * len(inputs), out_specs=[ANY] * le...  33.8 us
    all_gather x1, waiting for transfers between devices, per_device(): cot_group = lax.all_gather(later_cot, 'seq', axis=0, tiled=True)  19.4 us
    dot_general x4, matrix products, nn(): return jnp.dot(a, b, preferred_element_type=F32)  14.9 us
    pallas_call x1, Pallas kernels, attention_forward(): pl.pallas_call(forward_kernel, in_specs=[VMEM] * 4, out_specs=[VMEM] * 3,...  12.8 us
    unnamed x121, local copies, waits for them, and re-layouts  12 us
    dot_general x4, matrix products, tn(): lax.dot_general(a, b, (((0,), (0,)), ((), ())), preferred_element_type=F32)  11.4 us
  transfers between devices with their start and end apart: 2, of which 2 were waited for; matrix products, arithmetic and copies ran while one was open for 4% of the time, Pallas kernels for 16%

profile of v1, /device:TPU:0, one launch (start us, length us, event | category | flops | bytes accessed | tf_op | source)
XLA Modules:
  0.0 383.9 jit_solution(14934169136159354652)
XLA Ops:
  7.3 1.6 copy.56
  10.7 33.8 %shard_map.238 = (bf16[4,128,1024]{2,1,0:T(8,128)(2,1)}, bf16[8,128,768]{2,1,0:T(8,128)(2,1)}, bf16[128,1024]{1,0:T(8,128)(2,1)}) custom-call(bf16[128,1024]{1,0:T(8,128)(2,1)} %refs_0_.1, bf16[128,768]{1,0:T(8,128)(2,1)} %copy.57.refs_1_, bf16[4,128,1024]{2,1,0:T(8,128)(2,1)} %bitcast.161), custom_call_target="tpu_custom_call" | custom-call | tf_op jit(solution)/shard_map/pallas_call | solution.py:698
  44.5 2.2 pad_maximum_fusion
  55.8 24.3 %shard_map.239 = (bf16[4,64,512]{2,1,0:T(8,128)(2,1)}, bf16[8,128,512]{2,1,0:T(8,128)(2,1)}) custom-call(bf16[4,64,512]{2,1,0:T(8,128)(2,1)} %maximum_multiply_fusion.2.refs_0_, bf16[4,128,512]{2,1,0:T(8,128)(2,1)} %pad_maximum_fusion.2.refs_1_), custom_call_target="tpu_custom_call" | custom-call | tf_op jit(solution)/shard_map/pallas_call | solution.py:93
  82.8 12.8 %shard_map.240 = (bf16[4,64,512]{2,1,0:T(8,128)(2,1)S(1)}, f32[4,64,512]{2,1,0:T(8,128)S(1)}, f32[4,1,512]{2,1,0:T(1,128)S(1)}) custom-call(bf16[4,64,512]{2,1,0:T(8,128)(2,1)S(1)} %copy-done.4, bf16[8,128,512]{2,1,0:T(8,128)(2,1)S(1)} %copy-done.2, bf16[4,64,512]{2,1,0:T(8,128)(2,1)S(1)} %bitcast.136, bf16[8,64,512]{2,1,0:T(8,128)(2,1)S(1)} %bitcast.134), custom_call_target="tpu_custom_call" | custom-call | flops 4294967296 | bytes 8388608 | tf_op jit(solution)/shard_map/pallas_call | solution.py:142
  96.5 25.1 %shard_map.241 = bf16[16,64,512]{2,1,0:T(8,128)(2,1)} custom-call(bf16[4,64,512]{2,1,0:T(8,128)(2,1)} %copy-done.7), custom_call_target="tpu_custom_call" | custom-call | tf_op jit(solution)/shard_map/pallas_call | solution.py:93
  122.2 3.6 all-gather.3.cloned.1.call-done
  125.8 3.6 multiply_reduce_fusion
  130.9 4.2 %fusion.7 = f32[512,1024]{1,0:T(8,128)} fusion(bf16[512,1024]{1,0:T(8,128)(2,1)S(1)} %multiply_convert_fusion.3, bf16[1024,4096]{1,0:T(8,128)(2,1)} %all-gather.3.cloned.1.call-done), kind=kOutput, calls=%fused_computation.29 | convolution fusion | flops 1073741824 | bytes 5242880 | tf_op jit(solution)/shard_map/dot_general | solution.py:23
  135.1 19.4 %all-gather.5.cloned.1.call-done = bf16[512,1024]{1,0:T(8,128)(2,1)} async-done(((bf16[128,1024]{1,0:T(8,128)(2,1)}), bf16[512,1024]{1,0:T(8,128)(2,1)}) %all-gather.5.cloned.1.call-update) | async-done | bytes 1048592 | tf_op jit(solution)/shard_map/all_gather | solution.py:318
  154.5 3.3 fusion.15
  157.8 3.6 multiply_convert_fusion
  161.5 2.6 convolution_convert_fusion.1
  164.1 2.6 convolution_convert_fusion.2
  168.1 2.6 convolution_convert_fusion
  170.7 2.3 add_convert_fusion
  173.0 21.6 %shard_map.242 = (bf16[4,128,1024]{2,1,0:T(8,128)(2,1)}, bf16[4,4,32,1024]{3,2,1,0:T(8,128)(2,1)}, bf16[4,4,32,1024]{3,2,1,0:T(8,128)(2,1)}, bf16[4,128,1024]{2,1,0:T(8,128)(2,1)}) custom-call(bf16[4,128,1024]{2,1,0:T(8,128)(2,1)} %bitcast.158, bf16[4,4,2,32,1024]{4,3,2,1,0:T(8,128)(2,1)} %bitcast.140, bf16[4,4,2,32,1024]{4,3,2,1,0:T(8,128)(2,1)} %bitcast.142, ...), custom_call_target="tpu_custom_call" | custom-call | tf_op jit(solution)/shard_map/pallas_call | solution.py:93
  194.5 3.0 fusion.refs_10_
  198.9 3.2 convolution_convert_fusion.3
  202.0 3.2 fusion.28
  205.2 14.2 %shard_map.243 = (bf16[4,4,64,128]{3,2,1,0:T(8,128)(2,1)}, bf16[4,4,32,1024]{3,2,1,0:T(8,128)(2,1)}) custom-call(bf16[16,64,128]{2,1,0:T(8,128)(2,1)} %bitcast.169, bf16[4,4,2,32,1024]{4,3,2,1,0:T(8,128)(2,1)} %bitcast.138), custom_call_target="tpu_custom_call" | custom-call | tf_op jit(solution)/shard_map/pallas_call | solution.py:93
  219.4 2.8 fusion.1.refs_9_
  225.8 3.9 %fusion.23 = bf16[512,1024]{1,0:T(8,128)(2,1)} fusion(bf16[512,1024]{1,0:T(8,128)(2,1)S(1)} %copy-done.56, bf16[1024,4096]{1,0:T(8,128)(2,1)} %all-gather.3.cloned.1.call-done), kind=kOutput, calls=%fused_computation.45 | convolution fusion | flops 1074266112 | bytes 4194304 | tf_op jit(solution)/shard_map/dot_general | solution.py:23
  229.8 49.8 %shard_map.244 = (bf16[4,64,512]{2,1,0:T(8,128)(2,1)S(1)}, bf16[8,128,512]{2,1,0:T(8,128)(2,1)S(1)}, f32[2,8,256]{2,1,0:T(8,128)S(1)}, bf16[4,4,32,1024]{3,2,1,0...) custom-call(bf16[4,64,512]{2,1,0:T(8,128)(2,1)S(1)} %copy-done.5, ...), custom_call_target="tpu_custom_call" | custom-call | tf_op jit(solution)/shard_map/pallas_call | solution.py:515
  283.1 2.2 reduce_sum.305.refs_4_
  285.3 20.7 %shard_map.245 = (bf16[4,64,512]{2,1,0:T(8,128)(2,1)}, bf16[8,128,512]{2,1,0:T(8,128)(2,1)}, bf16[4,32,1024]{2,1,0:T(8,128)(2,1)}, bf16[4,32,1024]{2,1,0:T(8,128)(2,1)}, bf16[4,32,1024]{2,1,0:T(8,128)(2,1)}) custom-call(bf16[4,64,512]{2,1,0:T(8,128)(2,1)} %copy-done.8, bf16[8,128,512]{2,1,0:T(8,128)(2,1)} %copy-done.3, ...), custom_call_target="tpu_custom_call" | custom-call | tf_op jit(solution)/shard_map/pallas_call | solution.py:93
  310.7 2.2 convolution_convert_fusion.4
  312.9 2.0 convolution_convert_fusion.5
  317.9 23.2 %shard_map.246 = (bf16[4,128,1024]{2,1,0:T(8,128)(2,1)}, bf16[8,4,32,768]{3,2,1,0:T(8,128)(2,1)}) custom-call(bf16[4,128,1024]{2,1,0:T(8,128)(2,1)} %bitcast.162, bf16[4,8,32,768]{3,2,1,0:T(8,128)(2,1)} %bitcast.155), custom_call_target="tpu_custom_call" | custom-call | tf_op jit(solution)/shard_map/pallas_call | solution.py:93
  341.1 1.6 convert_reduce_fusion.1
  347.8 17.7 %shard_map.247 = (bf16[4,32,768]{2,1,0:T(8,128)(2,1)}, f32[32,8,128]{2,1,0:T(8,128)}) custom-call(bf16[4,32,768]{2,1,0:T(8,128)(2,1)} %reduce_sum.311.refs_0_, f32[32,8,128]{2,1,0:T(8,128)} %copy-done.33), custom_call_target="tpu_custom_call" | custom-call | tf_op jit(solution)/shard_map/pallas_call | solution.py:93
  375.0 1.8 add_convert_fusion.1
  (229 shorter events, 45.4 us)
Async XLA Ops:
  7.2 118.6 %all-gather.3.cloned.1.call-start = ((), (), s32[]{:S(2)}) async-start(), calls=%async_computation | async-start | bytes 9437184 | tf_op jit(solution)/shard_map/all_gather | solution.py:316
  7.2 37.2 %copy-start.39 = (bf16[128,1024]{1,0:T(8,128)(2,1)S(1)}, bf16[128,1024]{1,0:T(8,128)(2,1)}, u32[]{:S(2)}) copy-start(bf16[128,1024]{1,0:T(8,128)(2,1)} %param.35) | copy-start | bytes 786436
  44.5 3.3 copy-start.43
  46.7 107.8 %all-gather.5.cloned.1.call-start = ((), (), s32[]{:S(2)}) async-start(), calls=%async_computation.1 | async-start | bytes 1310720 | tf_op jit(solution)/shard_map/all_gather | solution.py:318
  48.1 3.4 copy-start.50
  48.1 3.6 copy-start.41
  49.2 4.8 %copy-start.10 = (f32[768,512]{1,0:T(8,128)}, f32[768,512]{1,0:T(8,128)S(1)}, u32[]{:S(2)}) copy-start(f32[768,512]{1,0:T(8,128)S(1)} %fusion.66) | copy-start | bytes 4718596
  49.2 4.6 %copy-start.44 = (f32[64]{0:T(128)S(1)}, f32[64]{0:T(128)}, u32[]{:S(2)}) copy-start(f32[64]{0:T(128)} %param.32) | copy-start | bytes 772
  49.2 4.6 %copy-start.45 = (f32[64]{0:T(128)S(1)}, f32[64]{0:T(128)}, u32[]{:S(2)}) copy-start(f32[64]{0:T(128)} %param.33) | copy-start | bytes 772
  54.0 26.1 %copy-start.35 = (bf16[8,8,512]{2,0,1:T(8,128)(2,1)S(1)}, bf16[8,8,512]{2,0,1:T(8,128)(2,1)}, u32[]{:S(2)}) copy-start(bf16[8,8,512]{2,0,1:T(8,128)(2,1)} %subtract_convert_fusion.2) | copy-start | bytes 196612
  82.8 13.5 %copy-start.18 = (bf16[128,1024]{1,0:T(8,128)(2,1)S(1)}, bf16[128,1024]{1,0:T(8,128)(2,1)}, u32[]{:S(2)}) copy-start(bf16[128,1024]{1,0:T(8,128)(2,1)} %refs_0_.1) | copy-start | bytes 786436
  96.5 32.9 %copy-start.48 = (f32[128]{0:T(128)}, f32[128]{0:T(128)S(1)}, u32[]{:S(2)}) copy-start(f32[128]{0:T(128)S(1)} %fusion.33) | copy-start | bytes 1540
  125.8 3.6 copy-start.42
  129.4 68.7 %copy-start.12 = (f32[512,1024]{1,0:T(8,128)}, f32[512,1024]{1,0:T(8,128)S(1)}, u32[]{:S(2)}) copy-start(f32[512,1024]{1,0:T(8,128)S(1)} %get-tuple-element.227) | copy-start | bytes 6291460
  154.5 3.4 copy-start.29
  154.5 3.4 copy-start.54
  161.5 6.6 %copy-start.55 = (bf16[512,1024]{1,0:T(8,128)(2,1)}, bf16[512,1024]{1,0:T(8,128)(2,1)S(1)}, u32[]{:S(2)}) copy-start(bf16[512,1024]{1,0:T(8,128)(2,1)S(1)} %get-tuple-element.194) | copy-start | bytes 3145732
  161.5 5.3 %slice-start = ((s8[8388608]{0:T(1024)(128)(4,1)}), s8[4194304]{0:T(1024)(128)(4,1)S(1)}, s32[]{:S(2)}) async-start(s8[8388608]{0:T(1024)(128)(4,1)} %bitcast.170), calls=%async_computation.2 | async-start | bytes 8388608
  194.5 3.1 copy-start.25
  198.9 6.3 %copy-start.15 = (f32[128,1024]{1,0:T(8,128)}, f32[128,1024]{1,0:T(8,128)S(1)}, u32[]{:S(2)}) copy-start(f32[128,1024]{1,0:T(8,128)S(1)} %subtract_add_fusion) | copy-start | bytes 1572868
  202.0 17.4 %copy-start.9 = (bf16[1024,1024]{1,0:T(8,128)(2,1)S(1)}, bf16[1024,1024]{1,0:T(8,128)(2,1)}, u32[]{:S(2)}) copy-start(bf16[1024,1024]{1,0:T(8,128)(2,1)} %convolution_convert_fusion.3) | copy-start | bytes 6291460
  225.8 3.9 %copy-start.5 = (bf16[4,64,512]{2,1,0:T(8,128)(2,1)S(1)}, bf16[4,64,512]{2,1,0:T(8,128)(2,1)}, u32[]{:S(2)}) copy-start(bf16[4,64,512]{2,1,0:T(8,128)(2,1)} %get-tuple-element.106.q_ref.refs_0_) | copy-start | bytes 786436
  225.8 3.9 %copy-start.6 = (bf16[4,4,64,128]{3,2,1,0:T(8,128)(2,1)S(1)}, bf16[4,4,64,128]{3,2,1,0:T(8,128)(2,1)}, u32[]{:S(2)}) copy-start(bf16[4,4,64,128]{3,2,1,0:T(8,128)(2,1)} %get-tuple-element.112.refs_4_) | copy-start | bytes 786436
  317.9 24.8 %copy-start.19 = (bf16[128,1024]{1,0:T(8,128)(2,1)S(1)}, bf16[128,1024]{1,0:T(8,128)(2,1)}, u32[]{:S(2)}) copy-start(bf16[128,1024]{1,0:T(8,128)(2,1)} %refs_0_.1) | copy-start | bytes 786436
  317.9 24.8 %copy-start.46 = (f32[128]{0:T(128)S(1)}, f32[128]{0:T(128)}, u32[]{:S(2)}) copy-start(f32[128]{0:T(128)} %add_rsqrt_fusion.2) | copy-start | bytes 1540
  342.7 24.8 %copy-start.37 = (bf16[4,32,1024]{2,1,0:T(8,128)(2,1)S(1)}, bf16[4,32,1024]{2,1,0:T(8,128)(2,1)}, u32[]{:S(2)}) copy-start(bf16[4,32,1024]{2,1,0:T(8,128)(2,1)} %get-tuple-element.132) | copy-start | bytes 786436
  342.7 24.8 %copy-start.38 = (bf16[4,32,1024]{2,1,0:T(8,128)(2,1)S(1)}, bf16[4,32,1024]{2,1,0:T(8,128)(2,1)}, u32[]{:S(2)}) copy-start(bf16[4,32,1024]{2,1,0:T(8,128)(2,1)} %get-tuple-element.133) | copy-start | bytes 786436
  365.5 3.8 copy-start.40
  367.6 3.9 %copy-start.49 = (f32[128]{0:T(128)S(1)}, f32[128]{0:T(128)}, u32[]{:S(2)}) copy-start(f32[128]{0:T(128)} %copy-done.48) | copy-start | bytes 1540
  367.6 4.6 %copy-start.16 = (f32[128,1024]{1,0:T(8,128)S(1)}, f32[128,1024]{1,0:T(8,128)}, u32[]{:S(2)}) copy-start(f32[128,1024]{1,0:T(8,128)} %copy-done.15) | copy-start | bytes 1572868
  369.3 3.9 %copy-start.36 = (bf16[4,32,1024]{2,1,0:T(8,128)(2,1)S(1)}, bf16[4,32,1024]{2,1,0:T(8,128)(2,1)}, u32[]{:S(2)}) copy-start(bf16[4,32,1024]{2,1,0:T(8,128)(2,1)} %get-tuple-element.131) | copy-start | bytes 786436
  369.5 4.4 %copy-start.21 = (bf16[4,128,1024]{2,1,0:T(8,128)(2,1)S(1)}, bf16[4,128,1024]{2,1,0:T(8,128)(2,1)}, u32[]{:S(2)}) copy-start(bf16[4,128,1024]{2,1,0:T(8,128)(2,1)} %get-tuple-element.134) | copy-start | bytes 3145732
  (29 other events, 50.1 us)
Sparse Core Ops, SparseCore 0:
  46.8 78.9 all-gather.2
  127.4 27.0 all-gather.4
